TPU v7x, 512 devices: a whole 4x8x8 slice. The times are simulated.
512 devices in a mesh: grp: 32 (over x, y), seq: 16 (over z, core).
Axes of the slice: x: 4, y: 8, z: 8, core: 2. Of those that a mesh axis runs over, the one named last changes fastest.
Arguments:
- tokens: bfloat16 [131072, 512], P(('grp', 'seq')), parts along dimension 0, may hold values from -6 to 6
- group_pos: int32 [32768], P('grp'), parts along dimension 0, may hold values from 0 to 4095, as said below
- log_decay: float32 [131072, 16], P(('grp', 'seq')), parts along dimension 0, may hold values from -1 to 0, as said below
- in_weight: bfloat16 [512, 2176], replicated, may hold values from -0.25 to 0.25
- norm_gain: float32 [1024], replicated, may hold values from 0.1 to 1.9
- out_weight: bfloat16 [1024, 512], replicated, may hold values from -0.1875 to 0.1875
- inner_gain: float32 [512], replicated, may hold values from 0.1 to 1.9
- qkv_weight: bfloat16 [16, 512, 192], P('seq'), may hold values from -1 to 1
- attn_out: bfloat16 [16, 64, 512], P('seq'), may hold values from -0.1875 to 0.1875
Outputs:
- result: bfloat16 [131072, 512], P(('grp', 'seq')), parts along dimension 0
There are 32 independent parts, one for each index of `grp`. A program takes and returns all parts, laid end to end along the dimension named above; an argument that names none is the same for every part. Nothing has to cross between parts.
Inputs may be any that keep to these rules, and one draw needn't show every extreme that they name: `group_pos`: strictly increasing. Each device's 256 positions hold at least one group start and at most 128; some device holds exactly 128. `log_decay`: negative at every position.
All inputs are finite; a program needn't handle non-finite values.
Results may differ from a plain program's by a relative error of at most 0.0061.
Values may be sent and summed in bfloat16 or wider, within the bound.
A program may use at most 64 MiB of HBM per device.

v0:
```python
import jax
import jax.numpy as jnp
from jax import lax
from jax.sharding import Mesh
from jax.sharding import PartitionSpec as P

SEQ = ("seq_0", "seq_1")
GRP_SEQ = ("grp", "seq_0", "seq_1")


def nothing_yet(shard, identity):
    return jax.tree.map(
        lambda part, zero: jnp.zeros_like(part) + jnp.asarray(zero, part.dtype), shard, identity
    )


def carried_in(shard, axes, combine, identity):
    before = start = nothing_yet(shard, identity)
    subtotal = shard
    for axis in reversed(axes):
        count, here = (lax.axis_size(axis), lax.axis_index(axis))
        pieces = jax.tree.map(lambda part: lax.all_gather(part, axis), subtotal)
        inside, subtotal = (start, start)
        for k in range(count):
            passed = k < here
            subtotal = combine(subtotal, jax.tree.map(lambda part: part[k], pieces))
            inside = jax.tree.map(lambda new, old: jnp.where(passed, new, old), subtotal, inside)
        before = combine(inside, before)
    return before


def in_blocks(shard, dim, count):
    lengths = shard.shape
    tiles = shard.reshape(*lengths[:dim], count, lengths[dim] // count, *lengths[dim + 1 :])
    return jnp.moveaxis(tiles, dim, 0)


def joined_along(tiles, dim):
    tiles = jnp.moveaxis(tiles, 0, dim)
    lengths = tiles.shape
    return tiles.reshape(*lengths[:dim], lengths[dim] * lengths[dim + 1], *lengths[dim + 2 :])


def turned_blocks(tiles, axes, order):
    inside = tiles.shape[1:]
    result = tiles.reshape(*(lax.axis_size(a) for a in axes), *inside)
    for k in order:
        result = lax.all_to_all(result, axes[k], k, k, tiled=True)
    return result.reshape(-1, *inside)


def stepwise_exchange(shard, axes, order, split_dim, concat_dim):
    tiles = in_blocks(shard, split_dim, lax.axis_size(axes))
    return joined_along(turned_blocks(tiles, axes, order), concat_dim)


def rms_norm(values, gain):
    return values * lax.rsqrt(jnp.mean(values * values, axis=-1, keepdims=True) + 1e-05) * gain


def attend(rows, w_qkv, index, valid):
    head_dim = w_qkv.shape[1] // 3
    qkv = jnp.dot(rows, w_qkv, preferred_element_type=jnp.float32).astype(jnp.bfloat16)
    query = qkv[:, :head_dim]
    keys = qkv[:, head_dim : 2 * head_dim]
    values = qkv[:, 2 * head_dim :]
    count = rows.shape[0]
    block = min(512, count)

    def one_block(start):
        query_block = lax.dynamic_slice_in_dim(query, start, block, 0)
        index_block = lax.dynamic_slice_in_dim(index, start, block, 0)
        scores = jnp.dot(query_block, keys.T, preferred_element_type=jnp.float32) * head_dim ** (
            -0.5
        )
        allowed = (index[None, :] <= index_block[:, None]) & valid[None, :]
        scores = jnp.where(allowed, scores, -jnp.inf)
        top = jnp.max(scores, axis=1, keepdims=True)
        expo = jnp.exp(scores - top)
        probs = (expo / jnp.sum(expo, axis=1, keepdims=True)).astype(jnp.bfloat16)
        return jnp.dot(probs, values, preferred_element_type=jnp.float32).astype(jnp.bfloat16)

    starts = jnp.arange(count // block, dtype=jnp.int32) * block
    return lax.map(one_block, starts).reshape(count, head_dim)


def shards(
    tokens, group_pos, log_decay, in_weight, norm_gain, out_weight, inner_gain, qkv_weight, attn_out
):
    highest = lax.Precision.HIGHEST
    length = tokens.shape[0]
    heads = log_decay.shape[1]
    width = out_weight.shape[0]
    model_width = out_weight.shape[1]
    head_size = width // heads
    state_dim = (in_weight.shape[1] - 2 * width) // 2
    proj = jnp.dot(tokens, in_weight, preferred_element_type=jnp.float32).astype(jnp.bfloat16)
    xs = proj[:, :width].astype(jnp.float32).reshape(length, heads, head_size)
    gate = proj[:, width : 2 * width].astype(jnp.float32)
    bmat = proj[:, 2 * width : 2 * width + state_dim].astype(jnp.float32)
    cmat = proj[:, 2 * width + state_dim :].astype(jnp.float32)
    cumul = jnp.cumsum(log_decay, axis=0)
    differ = cumul.T[:, :, None] - cumul.T[:, None, :]
    lower = jnp.arange(length)[:, None] >= jnp.arange(length)[None, :]
    decays = jnp.exp(jnp.where(lower[None], differ, -jnp.inf))
    intersections = jnp.dot(cmat, bmat.T, precision=highest)
    within = jnp.einsum("hij,jhp->ihp", decays * intersections[None], xs, precision=highest)
    tails = jnp.exp(cumul[-1][None, :] - cumul)
    local_state = jnp.einsum("jh,jhp,jn->hpn", tails, xs, bmat, precision=highest)
    total_decay = jnp.exp(cumul[-1])

    def link(earlier, later):
        return (earlier[0] * later[0], later[0][:, None, None] * earlier[1] + later[1])

    identity = (jnp.ones_like(total_decay), jnp.zeros_like(local_state))
    _, state_in = carried_in((total_decay, local_state), SEQ, link, identity)
    carried = jnp.einsum("ih,in,hpn->ihp", jnp.exp(cumul), cmat, state_in, precision=highest)
    gated = (within + carried).reshape(length, width) * jax.nn.silu(gate)
    normed = rms_norm(gated, norm_gain).astype(jnp.bfloat16)
    hidden = (
        tokens.astype(jnp.float32) + jnp.dot(normed, out_weight, preferred_element_type=jnp.float32)
    ).astype(jnp.bfloat16)
    position = lax.axis_index(SEQ)
    devices = lax.axis_size(SEQ)
    most = length // 2
    groups = group_pos.shape[0]
    starts = jnp.arange(devices, dtype=jnp.int32) * length
    before = jnp.sum((group_pos[None, :] < starts[:, None]).astype(jnp.int32), axis=1)
    upto = jnp.sum((group_pos[None, :] < (starts + length)[:, None]).astype(jnp.int32), axis=1)
    counts = upto - before
    slots = jnp.arange(most, dtype=jnp.int32)
    picks = jnp.clip(before[position] + slots, 0, groups - 1)
    valid_here = slots < counts[position]
    local_pos = group_pos[picks] - position * length
    placing = (
        (local_pos[:, None] == jnp.arange(length, dtype=jnp.int32)[None, :]) & valid_here[:, None]
    ).astype(jnp.float32)
    rows = jnp.dot(placing.astype(jnp.bfloat16), hidden, preferred_element_type=jnp.float32)
    rows_n = rms_norm(rows, inner_gain).astype(jnp.bfloat16)
    gathered = lax.all_gather(rows_n, SEQ, axis=0, tiled=True)
    slot_group = (before[:, None] + slots[None, :]).reshape(-1)
    slot_valid = (slots[None, :] < counts[:, None]).reshape(-1)
    w_qkv = qkv_weight[0]
    owners = group_pos // length
    ordinal = jnp.arange(groups, dtype=jnp.int32)
    index = owners * most + ordinal - before[owners]
    packed = jnp.take(gathered, index, axis=0)
    outputs = attend(packed, w_qkv, ordinal, jnp.ones((groups,), jnp.bool_))
    spread = jnp.take(outputs, jnp.clip(slot_group, 0, groups - 1), axis=0)
    heads_out = jnp.where(slot_valid[:, None], spread, jnp.zeros_like(spread))
    full_out = lax.all_gather(attn_out, SEQ, axis=0, tiled=True)
    mine = stepwise_exchange(heads_out[:, None, :], SEQ, (1, 0), 0, 1)
    back = jnp.dot(
        mine.reshape(most, -1),
        full_out.reshape(-1, model_width),
        preferred_element_type=jnp.float32,
    )
    placed = jnp.dot(placing.T, back, precision=highest)
    return (hidden.astype(jnp.float32) + placed).astype(jnp.bfloat16)


def solution(mesh):
    split = Mesh(mesh.devices.reshape(mesh.shape["grp"], 8, 2), ("grp", "seq_0", "seq_1"))
    return jax.shard_map(
        shards,
        mesh=split,
        in_specs=(
            P(GRP_SEQ, None),
            P("grp"),
            P(GRP_SEQ, None),
            P(),
            P(),
            P(),
            P(),
            P(SEQ, None, None),
            P(SEQ, None, None),
        ),
        out_specs=P(GRP_SEQ, None),
        check_vma=False,
    )
```

profile of v0, /device:TPU:2, one launch (start us, length us, event | category | flops | bytes accessed | tf_op | source)
XLA Modules:
  0.0 190.6 jit_solution(11118988941506550398)
XLA Ops:
  6.5 1.6 copy-done
  8.2 2.0 %convolution_convert_fusion.1 = bf16[256,2176]{0,1:T(8,128)(2,1)S(1)} fusion(bf16[256,512]{1,0:T(8,128)(2,1)} %param.11, bf16[512,2176]{1,0:T(8,128)(2,1)S(1)} %copy-done), kind=kOutput, calls=%fused_computation.17 | convolution fusion | flops 570982400 | bytes 3604480 | tf_op jit(solution)/shard_map/dot_general | solution.py:97
  10.1 0.8 slice.156
  11.0 0.6 reduce-window.6
  11.5 0.2 slice_reduce_fusion
  11.7 0.1 fusion.125
  11.8 0.2 exponential_reduce_fusion
  12.0 0.1 bitcast_exponential_fusion
  12.1 1.7 fusion.26
  13.8 2.7 %all-gather = f32[32,64,64]{2,1,0:T(8,128)} all-gather(f32[16,64,64]{2,1,0:T(8,128)S(1)} %fusion.26), channel_id=2, replica_groups=mesh['grp'=32,'seq_0'=8,'seq_1'=2] {'seq_1'}, dimensions={0}, use_global_device_ids=true | all-gather | bytes 786432 | tf_op jit(solution)/shard_map/all_gather | solution.py:22
  16.5 1.8 all-gather.1
  18.3 2.1 %bitcast_add_fusion = f32[1,16,64,64]{3,2,1,0:T(8,128)} fusion(f32[32,64,64]{2,1,0:T(8,128)} %all-gather, f32[16]{0:T(128)S(1)} %get-tuple-element.146, f32[16]{0:T(128)S(1)} %get-tuple-element.148), kind=kLoop, calls=%fused_computation.64 | loop fusion | flops 196608 | bytes 786560 | tf_op jit(solution)/shard_map/add | solution.py:113
  20.5 0.2 convert_reduce_fusion
  20.7 0.7 fusion.129
  21.5 0.7 fusion.120
  22.1 1.0 gather_fusion
  23.1 0.6 dynamic_slice.17
  23.7 22.2 %all-gather.2 = f32[8,1,16]{2,1,0:T(1,128)S(1)} all-gather(f32[1,1,16]{2,1,0:T(1,128)S(1)} %get-tuple-element.147), channel_id=1, replica_groups=mesh['grp'=32,'seq_0'=8,'seq_1'=2] {'seq_0'}, dimensions={0}, use_global_device_ids=true | all-gather | bytes 576 | tf_op jit(solution)/shard_map/all_gather | solution.py:22
  45.9 0.7 iota_compare_fusion.3
  46.7 0.2 fusion.110
  46.9 5.4 %fusion.15 = f32[256,16,64]{0,2,1:T(8,128)} fusion(bf16[256,16,64]{0,2,1:T(8,128)(2,1)} %bitcast.189, f32[256,256]{1,0:T(8,128)S(1)} %fusion.110, f32[16,256]{1,0:T(8,128)S(1)} %get-tuple-element.136, pred[256,256]{1,0:T(8,128)(4,1)S(1)} %iota_compare_fusion), kind=kOutput, calls=%fused_computation.23 | convolution fusion | flops 808452096 | bytes 1916928 | tf_op jit(solution)/shard_map/hij,jhp->ihp/dot_general | solution.py:107
  52.2 31.2 %all-gather.7.cloned.1.call-done = f32[8,16,64,64]{3,2,1,0:T(8,128)} async-done(((f32[1,16,64,64]{3,2,1,0:T(8,128)}), f32[8,16,64,64]{3,2,1,0:T(8,128)}) %all-gather.7.cloned.1.call-update) | async-done | bytes 2097168 | tf_op jit(solution)/shard_map/all_gather | solution.py:22
  83.5 4.5 %fusion.18 = f32[256,16,64]{0,2,1:T(8,128)S(1)} fusion(f32[256,16,64]{0,2,1:T(8,128)} %fusion.15, f32[8,16,64,64]{3,2,1,0:T(8,128)} %all-gather.7.cloned.1.call-done, f32[256,16]{0,1:T(8,128)S(1)} %get-tuple-element.133, f32[256,64]{0,1:T(8,128)S(1)} %slice_convert_fusion, f32[32,64,64]{2,1,0:T(8,128)} %all-gather, f32[16]{0:T(128)S(1)} %get-tuple-element.146, ...), kind=kOutput, calls=%fused_computation.25 | convolution fusion | flops 203816960 | bytes 4801226 | tf_op jit(solution)/shard_map/ih,in,hpn->ihp/dot_general | solution.py:117
  88.1 0.4 multiply_reduce_fusion
  88.5 0.5 copy-done.2
  89.0 0.4 copy-done.3
  89.3 0.8 fusion.19
  90.1 0.3 multiply_reduce_fusion.1
  90.5 0.8 multiply_convert_fusion.2
  91.3 0.7 all-gather.11.cloned.1.call-update
  92.1 0.1 reduce_sum.53
  92.1 0.1 reduce_sum.52
  92.2 10.1 %compare_and_fusion = (pred[1024]{0:T(1024)(128)(4,1)S(1)}, s32[1024]{0:T(1024)S(1)}) fusion(s32[]{:T(128)} %bitcast.45, s32[]{:T(128)} %bitcast.44, s32[]{:T(128)} %bitcast.43, s32[]{:T(128)} %bitcast.42, s32[]{:T(128)} %bitcast.41, s32[]{:T(128)} %bitcast.40, s32[]{:T(128)} %bitcast.39, s32[]{:T(128)} %bitcast.38, s32[]{:T(128)} %bitcast.37, s32[]{:T(128)} %bitcast.36, ...), kind=kLoop, calls=%fused_computation.165 | loop fusion | flops 58368 | bytes 9280 | tf_op jit(solution)/shard_map/jit(_take)/and | solution.py:147
  102.4 0.1 copy.78
  102.4 0.1 fusion.115
  102.5 0.1 copy.77
  102.6 0.1 iota_compare_fusion.2
  102.7 30.0 %all-gather.9.cloned.1.call-done = bf16[2048,512]{1,0:T(8,128)(2,1)} async-done(((bf16[128,512]{1,0:T(8,128)(2,1)}), bf16[2048,512]{1,0:T(8,128)(2,1)}) %all-gather.9.cloned.1.call-update) | async-done | bytes 2097168 | tf_op jit(solution)/shard_map/all_gather | solution.py:140
  132.7 7.0 %gather_fusion.1 = bf16[1024,512]{1,0:T(8,128)(2,1)} fusion(bf16[2048,512]{1,0:T(8,128)(2,1)} %all-gather.9.cloned.1.call-done, s32[1024]{0:T(1024)S(1)} %broadcast_clamp_fusion.1), kind=kCustom, calls=%fused_computation.1 | custom fusion | bytes 2101248 | tf_op jit(solution)/shard_map/jit(_take)/gather | solution.py:147
  139.6 1.8 convolution_convert_fusion.2
  141.4 0.7 fusion.128
  142.1 0.2 copy.80
  142.3 0.2 copy.81
  142.5 11.1 %while.11 = (s32[]{:T(128)}, bf16[2,512,64]{1,2,0:T(8,128)(2,1)S(1)}, s32[1024]{0:T(1024)S(1)}, s32[2]{0:T(128)S(1)}, bf16[1024,64]{0,1:T(8,128)(2,1)}, /*index=...) while((s32[]{:T(128)}, ...), condition=%wide.region_9.10_spmd.clone, body=%wide.region_6.9_spmd.clone.sunk | while | flops 138968064 | bytes 6836391 | solution.py:84
  142.5 0.7 dynamic_slice.30
  145.3 0.1 dynamic_slice.31
  145.3 1.6 fusion.149
  147.0 0.5 fusion.150
  147.5 0.6 fusion.151
  148.1 0.7 dynamic_slice.30
  150.8 0.1 dynamic_slice.31
  150.9 1.6 fusion.149
  152.5 0.5 fusion.150
  153.0 0.6 fusion.151
  153.6 0.2 copy.82
  153.8 6.2 %gather_fusion.2 = bf16[2048,64]{1,0:T(8,128)(2,1)S(1)} fusion(bf16[1024,64]{1,0:T(8,128)(2,1)S(1)} %bitcast.186, s32[2048]{0:T(1024)S(1)} %broadcast_clamp_fusion), kind=kCustom, calls=%fused_computation.2 | custom fusion | bytes 532480 | tf_op jit(solution)/shard_map/jit(_take)/gather | solution.py:149
  160.0 0.2 copy.83
  160.3 3.9 %all_to_all.10 = bf16[8,2,128,1,64]{2,4,3,0,1:T(8,128)(2,1)S(1)} all-to-all(bf16[8,2,128,1,64]{2,4,3,0,1:T(8,128)(2,1)S(1)} %select_select_fusion), channel_id=1, replica_groups=mesh['grp'=32,'seq_0'=8,'seq_1'=2] {'seq_1'}, dimensions={1} | all-to-all | bytes 524288 | tf_op jit(solution)/shard_map/all_to_all | solution.py:48
  164.2 0.7 copy.84
  165.0 4.2 %all-to-all-start.1 = ((bf16[8,2,128,1,64]{2,4,3,1,0:T(8,128)(2,1)}), bf16[8,2,128,1,64]{2,4,3,1,0:T(8,128)(2,1)S(1)}, u32[]{:S(2)}, u32[]{:S(2)}) async-start(bf16[8,2,128,1,64]{2,4,3,1,0:T(8,128)(2,1)} %copy.84), calls=%async_computation.1 | async-start | bytes 524288 | tf_op jit(solution)/shard_map/all_to_all | solution.py:48
  169.1 5.9 %all-gather.11.cloned.1.call-done = bf16[16,64,512]{2,1,0:T(8,128)(2,1)} async-done(((bf16[1,64,512]{2,1,0:T(8,128)(2,1)}), bf16[16,64,512]{2,1,0:T(8,128)(2,1)}) %all-gather.11.cloned.1.call-update) | async-done | bytes 1048592 | tf_op jit(solution)/shard_map/all_gather | solution.py:151
  175.0 6.3 %all-to-all-done.1 = bf16[8,2,128,1,64]{2,4,3,1,0:T(8,128)(2,1)S(1)} async-done(((bf16[8,2,128,1,64]{2,4,3,1,0:T(8,128)(2,1)}), bf16[8,2,128,1,64]{2,4,3,1,0:T(8,128)(2,1)S(1)}, u32[]{:S(2)}, u32[]{:S(2)}) %all-to-all-start.1) | async-done | bytes 262176 | tf_op jit(solution)/shard_map/all_to_all | solution.py:48
  181.3 1.6 fusion.130
  182.9 1.2 fusion.20
  (41 shorter events, 0.4 us)
Async XLA Ops:
  6.5 1.6 copy-start
  6.5 76.9 %all-gather.7.cloned.1.call-start = ((), (), s32[]{:S(2)}) async-start(), calls=%async_computation.2 | async-start | bytes 4718592 | tf_op jit(solution)/shard_map/all_gather | solution.py:22
  8.2 2.8 %copy-start.4 = (f32[256,16]{0,1:T(8,128)S(1)}, f32[256,16]{0,1:T(8,128)}, u32[]{:S(2)}) copy-start(f32[256,16]{0,1:T(8,128)} %param.13) | copy-start | bytes 49156
  13.8 6.7 %copy-start.1 = (s32[1024]{0:T(1024)S(1)}, s32[1024]{0:T(1024)}, u32[]{:S(2)}) copy-start(s32[1024]{0:T(1024)} %param.12) | copy-start | bytes 12292
  20.4 112.3 %all-gather.9.cloned.1.call-start = ((), (), s32[]{:S(2)}) async-start(), calls=%async_computation.3 | async-start | bytes 2228224 | tf_op jit(solution)/shard_map/all_gather | solution.py:140
  88.0 1.0 copy-start.2
  88.0 1.3 copy-start.3
  88.0 1.3 copy-start.5
  88.4 2.0 %copy-start.6 = (f32[512]{0:T(512)S(1)}, f32[512]{0:T(512)}, u32[]{:S(2)}) copy-start(f32[512]{0:T(512)} %param.17) | copy-start | bytes 6148
  91.2 83.7 %all-gather.11.cloned.1.call-start = ((), (), s32[]{:S(2)}) async-start(), calls=%async_computation.4 | async-start | bytes 1114112 | tf_op jit(solution)/shard_map/all_gather | solution.py:151
  102.7 36.9 %copy-start.7 = (bf16[1,512,192]{1,2,0:T(8,128)(2,1)S(1)}, bf16[1,512,192]{1,2,0:T(8,128)(2,1)}, u32[]{:S(2)}) copy-start(bf16[1,512,192]{1,2,0:T(8,128)(2,1)} %param.18) | copy-start | bytes 589828
  165.0 16.3 %all-to-all-start.1 = ((bf16[8,2,128,1,64]{2,4,3,1,0:T(8,128)(2,1)}), bf16[8,2,128,1,64]{2,4,3,1,0:T(8,128)(2,1)S(1)}, u32[]{:S(2)}, u32[]{:S(2)}) async-start(bf16[8,2,128,1,64]{2,4,3,1,0:T(8,128)(2,1)} %copy.84), calls=%async_computation.1 | async-start | bytes 524288 | tf_op jit(solution)/shard_map/all_to_all | solution.py:48
Sparse Core Ops, SparseCore 0:
  20.6 62.8 all-gather.6
  91.4 41.2 all-gather.8
  134.8 40.1 all-gather.10
where the time goes:
time: 191 us
  waiting for transfers between devices  74.1 us (39%)
  blocking collectives  30.6 us (16%)
  matrix products  23.9 us (13%)
  local copies, waits for them, and re-layouts  23.1 us (12%)
  other arithmetic  17 us (9%)
  between operations  13.4 us (7%)
  starting transfers between devices  4.24 us (2%)
  loops' own time  4.2 us (2%)
    all_gather x1, waiting for transfers between devices, carried_in(): pieces = jax.tree.map(lambda part: lax.all_gather(part, axis), subtotal)  31.2 us
    all_gather x1, waiting for transfers between devices, shards(): gathered = lax.all_gather(rows_n, SEQ, axis=0, tiled=True)  30 us
    all_gather x3, blocking collectives, carried_in(): pieces = jax.tree.map(lambda part: lax.all_gather(part, axis), subtotal)  26.7 us
    and x1, other arithmetic, shards(): packed = jnp.take(gathered, index, axis=0)  10.1 us
    gather x1, local copies, waits for them, and re-layouts, shards(): packed = jnp.take(gathered, index, axis=0)  6.95 us
    gather x2, local copies, waits for them, and re-layouts, shards(): spread = jnp.take(outputs, jnp.clip(slot_group, 0, groups - 1), axis=0)  6.42 us
    all_to_all x1, waiting for transfers between devices, turned_blocks(): result = lax.all_to_all(result, axes[k], k, k, tiled=True)  6.32 us
    all_gather x1, waiting for transfers between devices, shards(): full_out = lax.all_gather(attn_out, SEQ, axis=0, tiled=True)  5.87 us
  transfers between devices with their start and end apart: 4, of which 4 were waited for; matrix products, arithmetic and copies ran while one was open for 23% of the time, Pallas kernels for 0%

commit v1 on v0

--- a/solution.py
+++ b/solution.py
@@ -148,7 +148,12 @@
     outputs = attend(packed, w_qkv, ordinal, jnp.ones((groups,), jnp.bool_))
     spread = jnp.take(outputs, jnp.clip(slot_group, 0, groups - 1), axis=0)
     heads_out = jnp.where(slot_valid[:, None], spread, jnp.zeros_like(spread))
-    full_out = lax.all_gather(attn_out, SEQ, axis=0, tiled=True)
+    full_out = jnp.concatenate(
+        lax.all_to_all(
+            jnp.stack(tuple((attn_out for _ in range(lax.axis_size(SEQ)))), 0), SEQ, 0, 0
+        ),
+        0,
+    )
     mine = stepwise_exchange(heads_out[:, None, :], SEQ, (1, 0), 0, 1)
     back = jnp.dot(
         mine.reshape(most, -1),

time: 191 us -> 224 us (1.17)
  the two profiles are of different devices: /device:TPU:2 before, /device:TPU:1 now
where the time goes in v1:
time: 224 us; the launch traced here: 223 us
  waiting for transfers between devices  90.6 us (40%)
  blocking collectives  44.3 us (20%)
  local copies, waits for them, and re-layouts  26.7 us (12%)
  matrix products  20.7 us (9%)
  other arithmetic  18.6 us (8%)
  between operations  13.8 us (6%)
  starting transfers between devices  4.68 us (2%)
  loops' own time  3.69 us (2%)
    all_gather x1, waiting for transfers between devices, carried_in(): pieces = jax.tree.map(lambda part: lax.all_gather(part, axis), subtotal)  34.7 us
    all_gather x1, waiting for transfers between devices, shards(): gathered = lax.all_gather(rows_n, SEQ, axis=0, tiled=True)  29.6 us
    all_to_all x1, waiting for transfers between devices, shards(): lax.all_to_all(jnp.stack(tuple((attn_out for _ in range(lax.axis_size(SEQ...  26.3 us
    all_gather x3, blocking collectives, carried_in(): pieces = jax.tree.map(lambda part: lax.all_gather(part, axis), subtotal)  24.1 us
    all_to_all x2, blocking collectives, turned_blocks(): result = lax.all_to_all(result, axes[k], k, k, tiled=True)  20.2 us
    and x1, other arithmetic, shards(): packed = jnp.take(gathered, index, axis=0)  10.6 us
    gather x2, local copies, waits for them, and re-layouts, shards(): spread = jnp.take(outputs, jnp.clip(slot_group, 0, groups - 1), axis=0)  6.42 us
    gather x1, local copies, waits for them, and re-layouts, shards(): packed = jnp.take(gathered, index, axis=0)  5.85 us
  transfers between devices with their start and end apart: 3, of which 3 were waited for; matrix products, arithmetic and copies ran while one was open for 10% of the time, Pallas kernels for 0%

profile of v1, /device:TPU:1, one launch (start us, length us, event | category | flops | bytes accessed | tf_op | source)
XLA Modules:
  0.0 223.1 jit_solution(13182242072250976446)
XLA Ops:
  6.5 1.6 copy-done
  8.2 2.0 convolution_convert_fusion.1
  10.1 0.8 slice.156
  11.0 0.6 reduce-window.6
  11.5 0.2 slice_reduce_fusion
  11.8 0.2 exponential_reduce_fusion
  12.0 0.1 bitcast_exponential_fusion
  12.1 1.7 fusion.27
  13.8 9.2 %all-gather = f32[32,64,64]{2,1,0:T(8,128)} all-gather(f32[16,64,64]{2,1,0:T(8,128)S(1)} %fusion.27), channel_id=2, replica_groups=mesh['grp'=32,'seq_0'=8,'seq_1'=2] {'seq_1'}, dimensions={0}, use_global_device_ids=true | all-gather | bytes 786432 | tf_op jit(solution)/shard_map/all_gather | solution.py:22
  23.0 1.8 all-gather.1
  24.8 2.1 bitcast_add_fusion
  27.1 0.2 convert_reduce_fusion
  27.3 0.7 fusion.130
  28.0 0.7 fusion.121
  28.7 1.0 gather_fusion
  29.7 0.6 dynamic_slice.17
  30.3 13.1 %all-gather.2 = f32[8,1,16]{2,1,0:T(1,128)S(1)} all-gather(f32[1,1,16]{2,1,0:T(1,128)S(1)} %get-tuple-element.147), channel_id=1, replica_groups=mesh['grp'=32,'seq_0'=8,'seq_1'=2] {'seq_0'}, dimensions={0}, use_global_device_ids=true | all-gather | bytes 576 | tf_op jit(solution)/shard_map/all_gather | solution.py:22
  43.4 0.6 iota_compare_fusion.3
  44.1 0.2 fusion.111
  44.3 5.4 %fusion.15 = f32[256,16,64]{0,2,1:T(8,128)} fusion(bf16[256,16,64]{0,2,1:T(8,128)(2,1)} %bitcast.193, f32[256,256]{1,0:T(8,128)S(1)} %fusion.111, f32[16,256]{1,0:T(8,128)S(1)} %get-tuple-element.136, pred[256,256]{1,0:T(8,128)(4,1)S(1)} %iota_compare_fusion), kind=kOutput, calls=%fused_computation.23 | convolution fusion | flops 808452096 | bytes 1916928 | tf_op jit(solution)/shard_map/hij,jhp->ihp/dot_general | solution.py:107
  49.7 34.7 %all-gather.6.cloned.1.call-done = f32[8,16,64,64]{3,2,1,0:T(8,128)} async-done(((f32[1,16,64,64]{3,2,1,0:T(8,128)}), f32[8,16,64,64]{3,2,1,0:T(8,128)}) %all-gather.6.cloned.1.call-update) | async-done | bytes 2097168 | tf_op jit(solution)/shard_map/all_gather | solution.py:22
  84.3 4.5 %fusion.18 = f32[256,16,64]{0,2,1:T(8,128)S(1)} fusion(f32[256,16,64]{0,2,1:T(8,128)} %fusion.15, f32[8,16,64,64]{3,2,1,0:T(8,128)} %all-gather.6.cloned.1.call-done, f32[256,16]{0,1:T(8,128)S(1)} %get-tuple-element.133, f32[256,64]{0,1:T(8,128)S(1)} %slice_convert_fusion, f32[32,64,64]{2,1,0:T(8,128)} %all-gather, f32[16]{0:T(128)S(1)} %get-tuple-element.146, ...), kind=kOutput, calls=%fused_computation.25 | convolution fusion | flops 203816960 | bytes 4801226 | tf_op jit(solution)/shard_map/ih,in,hpn->ihp/dot_general | solution.py:117
  88.9 0.4 multiply_reduce_fusion
  89.3 0.5 copy-done.2
  89.8 0.4 copy-done.3
  90.2 0.8 fusion.19
  91.0 0.3 multiply_reduce_fusion.1
  91.3 0.7 multiply_convert_fusion.2
  92.1 0.1 reduce_sum.53
  92.2 0.1 reduce_sum.52
  92.3 0.1 copy.77
  92.4 0.1 copy.76
  92.5 0.5 iota_multiply_fusion
  93.0 0.1 fusion.116
  93.1 0.7 iota_compare_fusion.2
  93.7 10.6 %compare_and_fusion = (pred[1024]{0:T(1024)(128)(4,1)}, s32[1024]{0:T(1024)S(1)}) fusion(s32[]{:T(128)} %bitcast.45, s32[]{:T(128)} %bitcast.44, s32[]{:T(128)} %bitcast.43, s32[]{:T(128)} %bitcast.42, s32[]{:T(128)} %bitcast.41, s32[]{:T(128)} %bitcast.40, s32[]{:T(128)} %bitcast.39, s32[]{:T(128)} %bitcast.38, s32[]{:T(128)} %bitcast.37, s32[]{:T(128)} %bitcast.36, ...), kind=kLoop, calls=%fused_computation.167 | loop fusion | flops 58368 | bytes 9280 | tf_op jit(solution)/shard_map/jit(_take)/and | solution.py:147
  104.4 29.6 %all-gather.8.cloned.1.call-done = bf16[2048,512]{1,0:T(8,128)(2,1)} async-done(((bf16[128,512]{1,0:T(8,128)(2,1)}), bf16[2048,512]{1,0:T(8,128)(2,1)}) %all-gather.8.cloned.1.call-update) | async-done | bytes 2097168 | tf_op jit(solution)/shard_map/all_gather | solution.py:140
  134.0 5.8 %gather_fusion.1 = bf16[1024,512]{1,0:T(8,128)(2,1)S(1)} fusion(bf16[2048,512]{1,0:T(8,128)(2,1)} %all-gather.8.cloned.1.call-done, s32[1024]{0:T(1024)S(1)} %broadcast_clamp_fusion.1), kind=kCustom, calls=%fused_computation.1 | custom fusion | bytes 2101248 | tf_op jit(solution)/shard_map/jit(_take)/gather | solution.py:147
  139.9 1.5 convolution_convert_fusion.2
  141.4 0.2 copy.79
  141.6 0.2 copy.80
  141.8 11.4 %while.11 = (s32[]{:T(128)}, bf16[2,512,64]{1,2,0:T(8,128)(2,1)}, s32[1024]{0:T(1024)S(1)}, s32[2]{0:T(128)}, bf16[1024,64]{0,1:T(8,128)(2,1)S(1)}, /*index=5*/b...) while((s32[]{:T(128)}, bf16[2,512,64]{1,2,0:T(8,128)(2,1)}, ...), condition=%wide.region_9.10_spmd.clone, body=%wide.region_6.9_spmd.clone.sunk | while | flops 138968064 | bytes 8016095 | solution.py:84
  141.8 1.2 dynamic_slice.30
  144.8 0.1 dynamic_slice.31
  144.9 0.8 fusion.148
  145.7 0.5 fusion.149
  146.2 0.6 fusion.150
  146.9 0.6 copy-done.5
  147.5 1.2 dynamic_slice.30
  150.6 0.8 fusion.148
  151.4 0.5 fusion.149
  151.9 0.6 fusion.150
  152.6 0.6 copy-done.5
  153.2 1.1 copy.81
  154.3 6.2 %gather_fusion.2 = bf16[2048,64]{1,0:T(8,128)(2,1)S(1)} fusion(bf16[1024,64]{1,0:T(8,128)(2,1)S(1)} %bitcast.190, s32[2048]{0:T(1024)S(1)} %broadcast_clamp_fusion), kind=kCustom, calls=%fused_computation.2 | custom fusion | bytes 532480 | tf_op jit(solution)/shard_map/jit(_take)/gather | solution.py:149
  160.5 0.2 copy.82
  160.8 4.6 %all_to_all.15 = bf16[8,2,128,1,64]{2,4,0,3,1:T(8,128)(2,1)} all-to-all(bf16[8,2,128,1,64]{2,4,0,3,1:T(8,128)(2,1)S(1)} %select_select_fusion), channel_id=1, replica_groups=mesh['grp'=32,'seq_0'=8,'seq_1'=2] {'seq_1'}, dimensions={1} | all-to-all | bytes 524288 | tf_op jit(solution)/shard_map/all_to_all | solution.py:48
  165.4 1.1 stack.2
  166.5 4.6 %all-to-all-start.2 = ((bf16[16,1,64,512]{3,2,1,0:T(8,128)(2,1)}), bf16[16,1,64,512]{3,2,1,0:T(8,128)(2,1)S(1)}, u32[]{:S(2)}, u32[]{:S(2)}) async-start(bf16[16,1,64,512]{3,2,1,0:T(8,128)(2,1)} %stack.2), calls=%async_computation.2 | async-start | bytes 2097152 | tf_op jit(solution)/shard_map/all_to_all | solution.py:152
  171.1 1.7 copy.83
  172.8 26.3 %all-to-all-done.2 = bf16[16,1,64,512]{3,2,1,0:T(8,128)(2,1)S(1)} async-done(((bf16[16,1,64,512]{3,2,1,0:T(8,128)(2,1)}), bf16[16,1,64,512]{3,2,1,0:T(8,128)(2,1)S(1)}, u32[]{:S(2)}, u32[]{:S(2)}) %all-to-all-start.2) | async-done | bytes 1048608 | tf_op jit(solution)/shard_map/all_to_all | solution.py:152
  199.1 15.7 %all_to_all.16 = bf16[8,2,128,1,64]{2,4,1,3,0:T(8,128)(2,1)S(1)} all-to-all(bf16[8,2,128,1,64]{2,4,1,3,0:T(8,128)(2,1)} %copy.83), channel_id=1, replica_groups=mesh['grp'=32,'seq_0'=8,'seq_1'=2] {'seq_0'}, dimensions={0} | all-to-all | bytes 524288 | tf_op jit(solution)/shard_map/all_to_all | solution.py:48
  214.7 0.3 convolution_bitcast_fusion.1
  215.1 1.2 fusion.20
  (58 shorter events, 0.6 us)
Async XLA Ops:
  6.5 1.6 copy-start
  6.5 77.8 %all-gather.6.cloned.1.call-start = ((), (), s32[]{:S(2)}) async-start(), calls=%async_computation.3 | async-start | bytes 4718592 | tf_op jit(solution)/shard_map/all_gather | solution.py:22
  8.2 2.8 %copy-start.7 = (f32[256,16]{0,1:T(8,128)S(1)}, f32[256,16]{0,1:T(8,128)}, u32[]{:S(2)}) copy-start(f32[256,16]{0,1:T(8,128)} %param.13) | copy-start | bytes 49156
  13.8 13.3 %copy-start.1 = (s32[1024]{0:T(1024)S(1)}, s32[1024]{0:T(1024)}, u32[]{:S(2)}) copy-start(s32[1024]{0:T(1024)} %param.12) | copy-start | bytes 12292
  27.0 107.0 %all-gather.8.cloned.1.call-start = ((), (), s32[]{:S(2)}) async-start(), calls=%async_computation.4 | async-start | bytes 2228224 | tf_op jit(solution)/shard_map/all_gather | solution.py:140
  44.0 47.0 %copy-start.11 = (pred[128]{0:T(512)(128)(4,1)}, pred[128]{0:T(512)(128)(4,1)S(1)}, u32[]{:S(2)}) copy-start(pred[128]{0:T(512)(128)(4,1)S(1)} %iota_compare_fusion.3) | copy-start | bytes 388
  44.1 46.9 %copy-start.13 = (s32[128]{0:T(128)}, s32[128]{0:T(128)S(1)}, u32[]{:S(2)}) copy-start(s32[128]{0:T(128)S(1)} %broadcast_subtract_fusion) | copy-start | bytes 1540
  88.9 1.0 copy-start.2
  88.9 1.3 copy-start.3
  88.9 1.3 copy-start.9
  89.3 2.0 copy-start.10
  144.9 1.3 copy-start.4
  146.9 0.7 copy-start.5
  150.6 1.3 copy-start.4
  152.6 0.7 copy-start.5
  154.3 6.5 %copy-start.8 = (pred[8,2,128]{2,0,1:T(8,128)(4,1)S(1)}, pred[8,2,128]{2,0,1:T(8,128)(4,1)}, u32[]{:S(2)}) copy-start(pred[8,2,128]{2,0,1:T(8,128)(4,1)} %iota_compare_fusion.2) | copy-start | bytes 6148
  154.3 11.1 %copy-start.6 = (bf16[1,64,512]{2,1,0:T(8,128)(2,1)S(1)}, bf16[1,64,512]{2,1,0:T(8,128)(2,1)}, u32[]{:S(2)}) copy-start(bf16[1,64,512]{2,1,0:T(8,128)(2,1)} %param.19) | copy-start | bytes 196612
  166.5 48.6 %copy-start.12 = (pred[128]{0:T(512)(128)(4,1)S(1)}, pred[128]{0:T(512)(128)(4,1)}, u32[]{:S(2)}) copy-start(pred[128]{0:T(512)(128)(4,1)} %copy-done.11) | copy-start | bytes 388
  166.5 48.6 %copy-start.14 = (s32[128]{0:T(128)S(1)}, s32[128]{0:T(128)}, u32[]{:S(2)}) copy-start(s32[128]{0:T(128)} %copy-done.13) | copy-start | bytes 1540
  166.5 32.6 %all-to-all-start.2 = ((bf16[16,1,64,512]{3,2,1,0:T(8,128)(2,1)}), bf16[16,1,64,512]{3,2,1,0:T(8,128)(2,1)S(1)}, u32[]{:S(2)}, u32[]{:S(2)}) async-start(bf16[16,1,64,512]{3,2,1,0:T(8,128)(2,1)} %stack.2), calls=%async_computation.2 | async-start | bytes 2097152 | tf_op jit(solution)/shard_map/all_to_all | solution.py:152
Sparse Core Ops, SparseCore 0:
  27.1 57.1 all-gather.5
  92.2 41.7 all-gather.7
